TPU v7x, 128 devices: a whole 4x4x4 slice. The times are simulated.
128 devices in a mesh: dp: 16 (over y, x), tensor: 8 (over z, core).
Axes of the slice: x: 4, y: 4, z: 4, core: 2. Of those that a mesh axis runs over, the one named last changes fastest.
Arguments:
- inputs: bfloat16 [16384, 2048], P('dp'), may hold values from -6 to 6
- norm_gain: bfloat16 [2048], replicated, may hold values from 0.5 to 1.5
- norm_bias: bfloat16 [2048], replicated, may hold values from -3 to 3
- attn_weight: bfloat16 [3, 2048, 2048], P(None, None, 'tensor'), may hold values from -0.1875 to 0.1875
- attn_bias: bfloat16 [3, 2048], P(None, 'tensor'), may hold values from -3 to 3
- dense_weight: bfloat16 [2048, 2048], P('tensor'), may hold values from -1.5 to 1.5
- dense_bias: bfloat16 [2048], replicated, may hold values from -3 to 3
- expand_weight: bfloat16 [2048, 8192], P(None, 'tensor'), may hold values from -0.125 to 0.125
- expand_bias: bfloat16 [8192], P('tensor'), may hold values from -3 to 3
- shrink_weight: bfloat16 [8192, 2048], P('tensor'), may hold values from -0.0625 to 0.0625
- shrink_bias: bfloat16 [2048], replicated, may hold values from -3 to 3
- cotangent: bfloat16 [16384, 2048], P('dp'), may hold values from -6 to 6
Outputs:
- output: bfloat16 [16384, 2048], P('dp')
- input_grad: float32 [16384, 2048], P('dp')
- gain_grad: float32 [2048], P('dp')
- shift_grad: float32 [2048], P('dp')
- attn_weight_grad: float32 [3, 2048, 2048], P(None, 'dp', 'tensor')
- attn_bias_grad: float32 [3, 2048], P(None, ('tensor', 'dp'))
- dense_weight_grad: float32 [2048, 2048], P('tensor', 'dp')
- dense_bias_grad: float32 [2048], P('dp')
- expand_weight_grad: float32 [2048, 8192], P('dp', 'tensor')
- expand_bias_grad: float32 [8192], P(('tensor', 'dp'))
- shrink_weight_grad: float32 [8192, 2048], P('tensor', 'dp')
- shrink_bias_grad: float32 [2048], P('dp')
All inputs are finite; a program needn't handle non-finite values.
Results may differ from a plain program's by a relative error of at most 0.005.
The roundings to bfloat16 on the way count: a program that leaves them out, or rounds other values in their place, can miss the bound.
Values sent between devices are 32-bit elements; how exact they have to be, the bound alone decides.
A program may use at most 192 MiB of HBM per device.

v0:
```python
import functools

import jax
import jax.numpy as jnp
from jax import lax
from jax.experimental import pallas as pl
from jax.experimental.pallas import tpu as pltpu
from jax.sharding import PartitionSpec as P

HD = 64
ROT = 32
LENGTH = 1024
D = 2048
F32 = jnp.float32
BF16 = jnp.bfloat16
MESH = pl.DeviceIdType.MESH

rotary_base = 10000.0
norm_eps = 1e-05

UNITS = 16
UROWS = 128
BATCHES = 16
BROWS = 192
KX = 5
KZ = 6
TICKS = 21


def layer_kernel(
    x_ref, g_ref, n_ref, act_ref, att_ref, gh_ref, gp_ref, sw_ref, dw_ref, ew_ref, aw_ref,
    vec_ref,
    go_ref, gi_ref, f_ref, gs_ref,
    stream, turned, part, core_in, mine, zp, zd, zb, done,
    xp, xd, xb, mid, yp, yd, yb,
    xsend, xrecv, ysend, yrecv, csend, crecv, zsend, zrecv, gsend, grecv, ssend, srecv, lsem,
):
    dp = lax.axis_index("dp")
    tn = lax.axis_index("tensor")
    x, y, c, z = dp % 4, dp // 4, tn % 2, tn // 2

    def side(axis, sg):
        if axis == 0:
            return (y * 4 + (x + sg + 4) % 4, tn)
        if axis == 1:
            return (((y + sg + 4) % 4) * 4 + x, tn)
        if axis == 2:
            return (dp, ((z + sg + 4) % 4) * 2 + c)
        return (dp, z * 2 + 1 - c)

    SIDES = [(0, 1), (0, -1), (1, 1), (1, -1), (2, 1), (2, -1), (3, 0)]
    barrier = pltpu.get_barrier_semaphore()
    for axis, sg in SIDES:
        pl.semaphore_signal(barrier, inc=1, device_id=side(axis, sg), device_id_type=MESH)

    gs_ref[...] = jnp.zeros_like(gs_ref)

    def remote(src, dst, ssem, rsem, to):
        return pltpu.make_async_remote_copy(
            src_ref=src, dst_ref=dst, send_sem=ssem, recv_sem=rsem, device_id=to, device_id_type=MESH
        )

    SG = (1, -1)
    HALVES = (0, 1)

    def rows_of(b, h, hh):
        return pl.ds(pl.multiple_of((b % 4) * BROWS + h * 96 + hh * 48, 8), 48)

    def own_rows(b, h, piece, hh):
        return (
            stream.at[:, piece, rows_of(b, h, hh)]
            if h == 0
            else stream.at[piece, :, rows_of(b, h, hh)]
        )

    def first(kind, h, d, b):
        a = (x, y)[h]
        sg = SG[d]
        slot = b % KX
        sems = (xsend.at[kind, h, d, slot], xrecv.at[kind, h, d, slot], side(h, sg))
        if kind == 0:
            return remote(own_rows(b, h, (a + 2) % 4, d), xp.at[h, d, slot], *sems)
        if kind == 1:
            return remote(own_rows(b, h, (a + sg + 4) % 4, 1 - d), xd.at[h, d, slot], *sems)
        return remote(xp.at[h, d, slot], xb.at[h, d, slot], *sems)

    def second(kind, h, d, b):
        a = (y, x)[h]
        sg = SG[d]
        slot = b % KX
        sems = (ysend.at[kind, h, d, slot], yrecv.at[kind, h, d, slot], side(1 - h, sg))
        if kind == 0:
            return remote(mid.at[h, slot, (a + 2) % 4, pl.ds(d * 48, 48)], yp.at[h, d, slot], *sems)
        if kind == 1:
            return remote(
                mid.at[h, slot, (a + sg + 4) % 4, pl.ds((1 - d) * 48, 48)], yd.at[h, d, slot], *sems
            )
        return remote(yp.at[h, d, slot], yb.at[h, d, slot], *sems)

    def each(make, kinds, b):
        for kind in kinds:
            for h in HALVES:
                for d in (0, 1):
                    yield make(kind, h, d, b)

    def x0(b):
        for copy in each(first, (0, 1), b):
            copy.start()

    def x1(b):
        slot = b % KX
        for h in HALVES:
            for d in (0, 1):
                a = (x, y)[h]
                first(0, h, d, b).wait_recv()
                xp[h, d, slot] = xp[h, d, slot] + own_rows(b, h, (a + SG[d] + 4) % 4, d)[...]
                first(2, h, d, b).start()

    def x2(b):
        slot = b % KX
        for h in HALVES:
            a = (x, y)[h]
            for d in (0, 1):
                first(1, h, d, b).wait_recv()
                first(2, h, d, b).wait_recv()
            for hh in (0, 1):
                mid[h, slot, :, pl.ds(hh * 48, 48)] = (
                    own_rows(b, h, a, hh)[...] + xb[h, hh, slot] + xd[h, 1 - hh, slot]
                )
            for kind in (0, 1):
                for d in (0, 1):
                    second(kind, h, d, b).start()
        for copy in each(first, (0, 1, 2), b):
            copy.wait_send()

    def x3(b):
        slot = b % KX
        for h in HALVES:
            a = (y, x)[h]
            for d in (0, 1):
                second(0, h, d, b).wait_recv()
                yp[h, d, slot] = (
                    yp[h, d, slot] + mid[h, slot, (a + SG[d] + 4) % 4, pl.ds(d * 48, 48)]
                )
                second(2, h, d, b).start()

    def x4(b):
        slot = b % KX
        for h in HALVES:
            a = (y, x)[h]
            for d in (0, 1):
                second(1, h, d, b).wait_recv()
                second(2, h, d, b).wait_recv()
            for hh in (0, 1):
                at = pl.ds(pl.multiple_of(b * BROWS + h * 96 + hh * 48, 8), 48)
                f_ref[at] = mid[h, slot, a, pl.ds(hh * 48, 48)] + yb[h, hh, slot] + yd[h, 1 - hh, slot]
        for copy in each(second, (0, 1, 2), b):
            copy.wait_send()

    def zrows(u, piece, hh):
        return mine.at[u % 3, pl.ds(pl.multiple_of(piece * 16 + hh * 8, 8), 8)]

    def along(kind, d, u):
        sg = SG[d]
        slot = u % KZ
        sems = (zsend.at[kind, d, slot], zrecv.at[kind, d, slot], side(2, sg))
        if kind == 0:
            return remote(zrows(u, (z + 2) % 4, d), zp.at[d, slot], *sems)
        if kind == 1:
            return remote(zrows(u, (z + sg + 4) % 4, 1 - d), zd.at[d, slot], *sems)
        return remote(zp.at[d, slot], zb.at[d, slot], *sems)

    def cross(u):
        return remote(
            part.at[u % 2, pl.ds(pl.multiple_of((1 - c) * 64, 64), 64)],
            core_in.at[u % 2],
            csend.at[u % 2],
            crecv.at[u % 2],
            side(3, 0),
        )

    def grow(u, cc, piece, off, size):
        return pl.ds(pl.multiple_of((u % 8) * UROWS + cc * 64 + piece * 16 + off, 8), size)

    def gather1(ref, d, u):
        slot = u % KZ
        return remote(
            done.at[u % 2], ref.at[grow(u, c, z, 0, 16)], gsend.at[0, d, slot], grecv.at[0, d, slot],
            side(2, SG[d]),
        )

    def gather2(ref, d, u):
        slot = u % KZ
        at = grow(u, c, (z - SG[d] + 4) % 4, d * 8, 8)
        return remote(
            ref.at[at], ref.at[at], gsend.at[1, d, slot], grecv.at[1, d, slot], side(2, SG[d])
        )

    def twin(ref, k, u):
        slot = u % KZ
        at = grow(u, c, (z + (0, -1, 1, 2)[k] + 4) % 4, 0, 16)
        src = done.at[u % 2] if k == 0 else ref.at[at]
        return remote(src, ref.at[at], ssend.at[k, slot], srecv.at[k, slot], side(3, 0))

    def keep(ref, u):
        return pltpu.make_async_copy(done.at[u % 2], ref.at[grow(u, c, z, 0, 16)], lsem.at[u % 2])

    def on_ref(u, body):
        @pl.when(u < 8)
        def _():
            body(go_ref)

        @pl.when(u >= 8)
        def _():
            body(gi_ref)

    def z0(u):
        rows = pl.ds(pl.multiple_of((u % 8) * UROWS, UROWS), UROWS)

        @pl.when(u < 8)
        def _():
            @pl.loop(0, 4)
            def _(j):
                cols = pl.ds(pl.multiple_of(j * 512, 512), 512)
                part[u % 2, :, cols] = jnp.dot(
                    act_ref[rows, :], sw_ref[:, cols], preferred_element_type=F32
                ) + jnp.dot(att_ref[rows, :], dw_ref[:, cols], preferred_element_type=F32)

        @pl.when(u >= 8)
        def _():
            nt = (((1,), (1,)), ((), ()))

            @pl.loop(0, 4)
            def _(j):
                cols = pl.ds(pl.multiple_of(j * 512, 512), 512)
                total = lax.dot_general(
                    gh_ref[rows, :], ew_ref[cols, :], nt, preferred_element_type=F32
                )
                for k in range(3):
                    total += lax.dot_general(
                        gp_ref[k, rows, :], aw_ref[k, cols, :], nt, preferred_element_type=F32
                    )
                part[u % 2, :, cols] = total

        cross(u).start()

    def z1(u):
        cross(u).wait_recv()
        mine[u % 3] = part[u % 2, pl.ds(pl.multiple_of(c * 64, 64), 64)] + core_in[u % 2]
        for kind in (0, 1):
            for d in (0, 1):
                along(kind, d, u).start()

    def z2(u):
        slot = u % KZ
        for d in (0, 1):
            along(0, d, u).wait_recv()
            zp[d, slot] = zp[d, slot] + zrows(u, (z + SG[d] + 4) % 4, d)[...]
            along(2, d, u).start()
        cross(u).wait_send()

    def z3(u):
        slot = u % KZ
        for d in (0, 1):
            along(1, d, u).wait_recv()
            along(2, d, u).wait_recv()
        whole = jnp.concatenate(
            [zrows(u, z, hh)[...] + zb[hh, slot] + zd[1 - hh, slot] for hh in (0, 1)], axis=0
        )
        rows = pl.ds(pl.multiple_of((u % 8) * UROWS + c * 64 + z * 16, 16), 16)
        states = x_ref[rows, :].astype(F32)

        @pl.when(u < 8)
        def _():
            done[u % 2] = states + whole + vec_ref[1:2, :]

        @pl.when(u >= 8)
        def _():
            center = jnp.mean(states, axis=-1, keepdims=True)
            centred = states - center
            spread = jnp.mean(centred * centred, axis=-1, keepdims=True)
            r = lax.rsqrt(spread + norm_eps)
            zz = centred * r
            e = whole * vec_ref[0:1, :]
            done[u % 2] = g_ref[rows, :].astype(F32) + r * (
                e
                - jnp.mean(e, axis=-1, keepdims=True)
                - zz * jnp.mean(e * zz, axis=-1, keepdims=True)
            )
            gs_ref[0:1, :] += jnp.sum(whole * zz, axis=0, keepdims=True)
            gs_ref[1:2, :] += jnp.sum(whole, axis=0, keepdims=True)

        def send(ref):
            keep(ref, u).start()
            for d in (0, 1):
                gather1(ref, d, u).start()
            twin(ref, 0, u).start()

        on_ref(u, send)
        for kind in (0, 1, 2):
            for d in (0, 1):
                along(kind, d, u).wait_send()

    def z4(u):
        def body(ref):
            for d in (0, 1):
                gather1(ref, d, u).wait_recv()
                gather2(ref, d, u).start()
                twin(ref, 1 + d, u).start()
            keep(ref, u).wait()
            for d in (0, 1):
                gather1(ref, d, u).wait_send()
            twin(ref, 0, u).wait_send()

        on_ref(u, body)

    def z5(u):
        def body(ref):
            for d in (0, 1):
                gather2(ref, d, u).wait_recv()
            twin(ref, 3, u).start()
            for d in (0, 1):
                gather2(ref, d, u).wait_send()
                twin(ref, 1 + d, u).wait_send()

        on_ref(u, body)

    def z6(u):
        def body(ref):
            twin(ref, 3, u).wait_send()
            for k in range(4):
                twin(ref, k, u).wait_recv()

        on_ref(u, body)

    def product(left, right, j):
        turned[...] = left.T
        at = pl.ds(pl.multiple_of((j % 3) * 256, 256), 256)

        @pl.loop(0, 8)
        def _(q):
            both = jnp.dot(
                turned[...],
                right[:, pl.ds(pl.multiple_of(q * 256, 256), 256)],
                preferred_element_type=F32,
            )
            for k in (0, 1):
                stream[q // 2, (q % 2) * 2 + k, at] = both[:, k * 128 : (k + 1) * 128]

    def block(j):
        @pl.when(j < 4)
        def _():
            product(act_ref[:, pl.ds(pl.multiple_of(j % 4 * 256, 256), 256)], g_ref, j)

        @pl.when((j >= 4) & (j < 8))
        def _():
            product(gh_ref[:, pl.ds(pl.multiple_of(j % 4 * 256, 256), 256)], n_ref, j)

        @pl.when(j == 8)
        def _():
            product(att_ref[...], g_ref, j)

        @pl.when(j > 8)
        def _():
            product(gp_ref[j - 9], n_ref, j)

    def within(i, n):
        return (i >= 0) & (i < n)

    pl.semaphore_wait(barrier, len(SIDES))

    @pl.loop(0, TICKS)
    def _(t):
        b = t - 1
        pl.when(within(t, UNITS))(lambda: z0(t))

        @pl.when(within(b, BATCHES))
        def _():
            @pl.when(b % 4 < 3)
            def _():
                block((b // 4) * 3 + b % 4)

            x0(b)

        pl.when(within(t, UNITS))(lambda: z1(t))
        pl.when(within(t - 2, BATCHES))(lambda: x1(t - 2))
        pl.when(within(t - 1, UNITS))(lambda: z2(t - 1))
        pl.when(within(t - 3, BATCHES))(lambda: x2(t - 3))
        pl.when(within(t - 2, UNITS))(lambda: z3(t - 2))
        pl.when(within(t - 4, BATCHES))(lambda: x3(t - 4))
        pl.when(within(t - 3, UNITS))(lambda: z4(t - 3))
        pl.when(within(t - 5, BATCHES))(lambda: x4(t - 5))
        pl.when(within(t - 4, UNITS))(lambda: z5(t - 4))
        pl.when(within(t - 5, UNITS))(lambda: z6(t - 5))


def run_layer(x, g, normed, act, att, gh, gp, sw, dw, ew, aw, vec):
    vmem = pl.BlockSpec(memory_space=pltpu.VMEM)
    anym = pl.BlockSpec(memory_space=pl.ANY)
    dma = pltpu.SemaphoreType.DMA
    return pl.pallas_call(
        layer_kernel,
        out_shape=(
            jax.ShapeDtypeStruct((LENGTH, D), F32),
            jax.ShapeDtypeStruct((LENGTH, D), F32),
            jax.ShapeDtypeStruct((3072, 128), F32),
            jax.ShapeDtypeStruct((8, D), F32),
        ),
        in_specs=[vmem] * 12,
        out_specs=(anym, anym, vmem, vmem),
        scratch_shapes=[
            pltpu.VMEM((4, 4, 4 * BROWS, 128), F32),
            pltpu.VMEM((256, LENGTH), BF16),
            pltpu.VMEM((2, UROWS, D), F32),
            pltpu.VMEM((2, 64, D), F32),
            pltpu.VMEM((3, 64, D), F32),
            pltpu.VMEM((2, KZ, 8, D), F32),
            pltpu.VMEM((2, KZ, 8, D), F32),
            pltpu.VMEM((2, KZ, 8, D), F32),
            pltpu.VMEM((2, 16, D), F32),
            pltpu.VMEM((2, 2, KX, 4, 48, 128), F32),
            pltpu.VMEM((2, 2, KX, 4, 48, 128), F32),
            pltpu.VMEM((2, 2, KX, 4, 48, 128), F32),
            pltpu.VMEM((2, KX, 4, 96, 128), F32),
            pltpu.VMEM((2, 2, KX, 48, 128), F32),
            pltpu.VMEM((2, 2, KX, 48, 128), F32),
            pltpu.VMEM((2, 2, KX, 48, 128), F32),
            dma((3, 2, 2, KX)),
            dma((3, 2, 2, KX)),
            dma((3, 2, 2, KX)),
            dma((3, 2, 2, KX)),
            dma((2,)),
            dma((2,)),
            dma((3, 2, KZ)),
            dma((3, 2, KZ)),
            dma((2, 2, KZ)),
            dma((2, 2, KZ)),
            dma((4, KZ)),
            dma((4, KZ)),
            dma((2,)),
        ],
        compiler_params=pltpu.CompilerParams(
            collective_id=0, has_side_effects=True, vmem_limit_bytes=62 << 20
        ),
        cost_estimate=pl.CostEstimate(flops=20 << 30, bytes_accessed=60 << 20, transcendentals=0),
    )(x, g, normed, act, att, gh, gp, sw, dw, ew, aw, vec)


def layer_norm(values, gain, shift):
    center = jnp.mean(values, axis=-1, keepdims=True)
    centred = values - center
    spread = jnp.mean(centred * centred, axis=-1, keepdims=True)
    return centred * lax.rsqrt(spread + norm_eps) * gain + shift


def gelu_tanh(values):
    return (
        0.5
        * values
        * (1.0 + jnp.tanh(0.7978845608 * (values + 0.044715 * values * values * values)))
    )


def rotary_tables(length, rot_dims):
    halfway = rot_dims // 2
    powers = jnp.arange(halfway).astype(jnp.float32) * (2.0 / rot_dims)
    freqs = jnp.exp(-powers * jnp.log(jnp.float32(rotary_base)))
    angles = jnp.arange(length).astype(jnp.float32)[:, None] * freqs[None, :]
    angles = jnp.concatenate([angles, angles], axis=1)
    return (jnp.cos(angles), jnp.sin(angles))


def rotate_heads(heads, cosine, sine, rot_dims):
    halfway = rot_dims // 2
    turned_part = heads[..., :rot_dims]
    swapped = jnp.concatenate([-turned_part[..., halfway:], turned_part[..., :halfway]], axis=-1)
    result = turned_part * cosine[:, None, :] + swapped * sine[:, None, :]
    return jnp.concatenate([result, heads[..., rot_dims:]], axis=-1)


def per_device(
    inputs,
    norm_gain,
    norm_bias,
    attn_weight,
    attn_bias,
    dense_weight,
    dense_bias,
    expand_weight,
    expand_bias,
    shrink_weight,
    shrink_bias,
    cotangent,
):
    tok_rows = inputs.shape[0]
    local_width = attn_weight.shape[2]
    local_heads = local_width // HD
    sequences = tok_rows // LENGTH
    row_block = min(512, LENGTH)
    factor = HD ** (-0.5)
    states = inputs.astype(jnp.float32)
    normed_full, norm_back = jax.vjp(
        layer_norm, states, norm_gain.astype(jnp.float32), norm_bias.astype(jnp.float32)
    )
    normed = normed_full.astype(jnp.bfloat16)
    proj = jnp.einsum("td,kde->kte", normed, attn_weight, preferred_element_type=jnp.float32)
    proj = (proj + attn_bias.astype(jnp.float32)[:, None, :]).reshape(
        3, sequences, LENGTH, local_heads, HD
    )
    cosine, sine = rotary_tables(LENGTH, ROT)

    def turn_heads(heads):
        return rotate_heads(heads, cosine, sine, ROT)

    query_full, query_back = jax.vjp(turn_heads, proj[0])
    key_full, key_back = jax.vjp(turn_heads, proj[1])
    query = query_full.astype(jnp.bfloat16)
    keys = key_full.astype(jnp.bfloat16)
    values = proj[2].astype(jnp.bfloat16)
    pieces = []
    log_totals = []
    for start_row in range(0, LENGTH, row_block):
        stop_row = start_row + row_block
        query_rows = query[:, start_row:stop_row]
        scores = (
            jnp.einsum(
                "sqhd,skhd->shqk",
                query_rows,
                keys[:, :stop_row],
                preferred_element_type=jnp.float32,
            )
            * factor
        )
        allowed = jnp.arange(stop_row)[None, :] <= (start_row + jnp.arange(row_block))[:, None]
        scores = jnp.where(allowed, scores, -1e30)
        row_top = jnp.max(scores, axis=-1, keepdims=True)
        expo = jnp.exp(scores - row_top)
        row_total = jnp.sum(expo, axis=-1, keepdims=True)
        chances = (expo / row_total).astype(jnp.bfloat16)
        pieces.append(
            jnp.einsum(
                "shqk,skhd->sqhd", chances, values[:, :stop_row], preferred_element_type=jnp.float32
            )
        )
        log_totals.append(row_top + jnp.log(row_total))
    attended = jnp.concatenate(pieces, axis=1).reshape(tok_rows, local_width).astype(jnp.bfloat16)
    hidden = jnp.dot(
        normed, expand_weight, preferred_element_type=jnp.float32
    ) + expand_bias.astype(jnp.float32)
    act_full, gelu_back = jax.vjp(gelu_tanh, hidden)
    act = act_full.astype(jnp.bfloat16)
    grad_full = cotangent.astype(jnp.float32)
    bias_term = jnp.sum(grad_full, axis=0)
    grad_act = jnp.einsum("td,fd->tf", cotangent, shrink_weight, preferred_element_type=jnp.float32)
    grad_hidden = gelu_back(grad_act)[0].astype(jnp.bfloat16)
    expand_bias_term = jnp.sum(grad_hidden.astype(jnp.float32), axis=0)
    grad_att = jnp.einsum("td,ed->te", cotangent, dense_weight, preferred_element_type=jnp.float32)
    grad_att = grad_att.astype(jnp.bfloat16).reshape(sequences, LENGTH, local_heads, HD)
    grad_query_parts = []
    grad_keys = jnp.zeros((sequences, LENGTH, local_heads, HD), jnp.float32)
    grad_values = jnp.zeros((sequences, LENGTH, local_heads, HD), jnp.float32)
    for number, start_row in enumerate(range(0, LENGTH, row_block)):
        stop_row = start_row + row_block
        query_rows = query[:, start_row:stop_row]
        key_rows = keys[:, :stop_row]
        value_rows = values[:, :stop_row]
        grad_rows = grad_att[:, start_row:stop_row]
        scores = (
            jnp.einsum("sqhd,skhd->shqk", query_rows, key_rows, preferred_element_type=jnp.float32)
            * factor
        )
        allowed = jnp.arange(stop_row)[None, :] <= (start_row + jnp.arange(row_block))[:, None]
        chances = jnp.where(allowed, jnp.exp(scores - log_totals[number]), 0.0)
        grad_chances = jnp.einsum(
            "sqhd,skhd->shqk", grad_rows, value_rows, preferred_element_type=jnp.float32
        )
        row_dot = jnp.sum(chances * grad_chances, axis=-1, keepdims=True)
        grad_scores = (chances * (grad_chances - row_dot)).astype(jnp.bfloat16)
        grad_query_parts.append(
            jnp.einsum("shqk,skhd->sqhd", grad_scores, key_rows, preferred_element_type=jnp.float32)
            * factor
        )
        padding = ((0, 0), (0, LENGTH - stop_row), (0, 0), (0, 0))
        grad_keys = grad_keys + jnp.pad(
            jnp.einsum(
                "shqk,sqhd->skhd", grad_scores, query_rows, preferred_element_type=jnp.float32
            )
            * factor,
            padding,
        )
        grad_values = grad_values + jnp.pad(
            jnp.einsum(
                "shqk,sqhd->skhd",
                chances.astype(jnp.bfloat16),
                grad_rows,
                preferred_element_type=jnp.float32,
            ),
            padding,
        )
    grad_query_pre = query_back(jnp.concatenate(grad_query_parts, axis=1))[0]
    grad_key_pre = key_back(grad_keys)[0]
    grad_proj = (
        jnp.stack([grad_query_pre, grad_key_pre, grad_values])
        .reshape(3, tok_rows, local_width)
        .astype(jnp.bfloat16)
    )
    attn_bias_term = jnp.sum(grad_proj.astype(jnp.float32), axis=1)
    vec = jnp.concatenate(
        [
            norm_gain.astype(F32)[None],
            (dense_bias.astype(F32) + shrink_bias.astype(F32))[None],
            jnp.zeros((6, D), F32),
        ]
    )
    summed, input_grad, pieces, sums = run_layer(
        inputs, cotangent, normed, act, attended, grad_hidden, grad_proj,
        shrink_weight, dense_weight, expand_weight, attn_weight, vec,
    )
    output = summed.astype(BF16)
    shrink_sum = pieces[:1024]
    expand_sum = pieces[1024:2048].T
    dense_sum = pieces[2048:2304]
    attn_sum = jnp.swapaxes(pieces[2304:].reshape(3, 256, 128), 1, 2)
    both = lax.psum(sums[:2], "tensor")
    gain_sum, shift_sum, bias_sum = lax.psum_scatter(
        jnp.concatenate([both, bias_term[None]]), "dp", scatter_dimension=1, tiled=True
    )
    attn_bias_sum = lax.psum_scatter(attn_bias_term, "dp", scatter_dimension=1, tiled=True)
    expand_bias_sum = lax.psum_scatter(expand_bias_term, "dp", scatter_dimension=0, tiled=True)
    return (
        output, input_grad, gain_sum, shift_sum, attn_sum, attn_bias_sum, dense_sum, bias_sum,
        expand_sum, expand_bias_sum, shrink_sum, bias_sum,
    )


def solution(mesh):
    placed = (
        P("dp", None),
        P(),
        P(),
        P(None, None, "tensor"),
        P(None, "tensor"),
        P("tensor", None),
        P(),
        P(None, "tensor"),
        P("tensor"),
        P("tensor", None),
        P(),
        P("dp", None),
    )
    return jax.shard_map(
        per_device,
        mesh=mesh,
        in_specs=placed,
        out_specs=(
            P("dp", None),
            P("dp", None),
            P("dp"),
            P("dp"),
            P(None, "dp", "tensor"),
            P(None, ("tensor", "dp")),
            P("tensor", "dp"),
            P("dp"),
            P("dp", "tensor"),
            P(("tensor", "dp")),
            P("tensor", "dp"),
            P("dp"),
        ),
        check_vma=False,
    )
```

profile of v0, /device:TPU:0, one launch (start us, length us, event | category | flops | bytes accessed | tf_op | source)
XLA Modules:
  0.0 369.3 jit_solution(15189176504929210614)
XLA Ops:
  7.4 0.8 convert_element_type.140
  8.2 3.1 convert_reduce_fusion
  11.4 1.2 fusion.2
  12.7 2.0 fusion.5.n_ref
  14.7 3.6 add_bitcast_fusion
  18.8 1.9 copy-done.3
  20.7 1.2 convert_reduce_fusion.1
  22.3 1.3 convolution_convert_fusion
  23.8 0.9 select_reduce_fusion.1
  24.7 0.9 fusion.20
  25.7 2.0 fusion.47
  27.7 1.0 fusion.39
  28.7 1.5 multiply_reduce_fusion.1
  30.2 1.6 multiply_convert_fusion.1
  32.4 0.8 fusion.43
  33.2 0.6 convert_element_type.138
  34.1 6.1 %fusion.90 = f32[1024,1024]{1,0:T(8,128)} fusion(bf16[1024,2048]{1,0:T(8,128)(2,1)S(1)} %fusion.5.n_ref, bf16[2048,1024]{1,0:T(8,128)(2,1)S(1)} %copy-done.16), kind=kOutput, calls=%fused_computation.146 | convolution fusion | flops 4294967296 | bytes 12582912 | tf_op jit(solution)/shard_map/dot_general | solution.py:547
  40.2 1.7 select_reduce_fusion
  41.9 2.4 fusion.6
  44.3 3.8 %fusion.48 = bf16[1,512,4,64]{1,3,2,0:T(8,128)(2,1)} fusion(bf16[1024,4,64]{0,2,1:T(8,128)(2,1)S(1)} %bitcast.131, f32[4,512,1024]{2,1,0:T(8,128)S(1)} %get-tuple-element.89, f32[4,512]{1,0:T(4,128)S(1)} %fusion.6, f32[4,512]{1,0:T(4,128)S(1)} %get-tuple-element.88, pred[512,1024]{1,0:T(8,128)(4,1)S(1)} %iota_compare_fusion), kind=kOutput, calls=%fused_computation.66 | convolution fusion | flops 279052288 | bytes 9715712 | tf_op jit(solution)/shard_map/shqk,skhd->sqhd/dot_general | solution.py:541
  48.1 6.1 %multiply_reduce_fusion = (f32[4,512]{1,0:T(4,128)}, f32[4,512,1024]{2,1,0:T(8,128)}) fusion(f32[4,512,1024]{2,1,0:T(8,128)S(1)} %get-tuple-element.89, f32[4,512]{1,0:T(4,128)S(1)} %log_add_fusion, pred[512,1024]{1,0:T(8,128)(4,1)S(1)} %iota_compare_fusion, bf16[1024,4,64]{0,2,1:T(8,128)(2,1)S(1)} %bitcast.132, bf16[1,1024,4,64]{1,3,2,0:T(8,128)(2,1)S(1)} %bitcast.142), kind=kOutput, calls=%fused_computation.10 | convolution fusion | flops 278919168 | bytes 18104320 | tf_op jit(solution)/shard_map/sqhd,skhd->shqk/dot_general | solution.py:574
  54.2 2.0 fusion.36
  56.4 1.1 pad_maximum_fusion.3
  57.5 1.0 copy.54.att_ref
  58.5 7.3 %multiply_convert_fusion = bf16[4,512,1024]{2,1,0:T(8,128)(2,1)S(1)} fusion(f32[4,512,1024]{2,1,0:T(8,128)} %get-tuple-element.95, f32[4,512,1024]{2,1,0:T(8,128)} %copy-done, f32[4,512]{1,0:T(4,128)} %get-tuple-element.94, f32[4,512]{1,0:T(4,128)S(1)} %log_add_fusion, pred[512,1024]{1,0:T(8,128)(4,1)S(1)} %iota_compare_fusion), kind=kLoop, calls=%fused_computation.9 | loop fusion | flops 12582912 | bytes 21512192 | tf_op jit(solution)/shard_map/convert_element_type | solution.py:578
  65.8 1.4 fusion.42
  67.2 0.9 fusion.32
  69.3 0.7 maximum_maximum_fusion.vec_ref
  70.0 13.0 %convert_reduce_fusion.2 = (f32[1024]{0:T(1024)S(1)}, bf16[1024,1024]{1,0:T(8,128)(2,1)}, bf16[1024,1024]{1,0:T(8,128)(2,1)}) fusion(f32[1024,1024]{1,0:T(8,128)} %fusion.90, f32[1024]{0:T(1024)S(1)} %copy-done.11, bf16[1024,2048]{1,0:T(8,128)(2,1)} %g_ref.1, bf16[1024,2048]{1,0:T(8,128)(2,1)} %sw_ref.1), kind=kOutput, calls=%fused_computation.29 | convolution fusion | flops 4325374976 | bytes 16785408 | tf_op jit(solution)/shard_map/td,fd->tf/dot_general | solution.py:554
  83.0 1.5 convert_reduce_fusion.3
  84.5 169.9 %shard_map.211 = (f32[1024,2048]{1,0:T(8,128)}, f32[1024,2048]{1,0:T(8,128)}, f32[3072,128]{1,0:T(8,128)}, f32[8,2048]{1,0:T(8,128)}) custom-call(bf16[1024,2048]{1,0:T(8,128)(2,1)} %x_ref.1, bf16[1024,2048]{1,0:T(8,128)(2,1)} %g_ref.1, bf16[1024,2048]{1,0:T(8,128)(2,1)} %copy-done.2, bf16[1024,1024]{1,0:T(8,128)(2,1)} %get-tuple-element.62.act_ref, ...), custom_call_target="tpu_custom_call" | custom-call | flops 21474836480 | bytes 62914560 | tf_op jit(solution)/shard_map/pallas_call | solution.py:401
  254.4 0.9 slice.95
  255.2 25.8 %psum.7 = f32[2,2048]{1,0:T(2,128)S(1)} all-reduce(f32[2,2048]{1,0:T(2,128)S(1)} %slice.95), channel_id=1, replica_groups=mesh['dp'=16,'tensor'=8] {'tensor'}, use_global_device_ids=true, to_apply=%region_8.9 | all-reduce | flops 4096 | bytes 32768 | tf_op jit(solution)/shard_map/psum | solution.py:624
  281.1 1.3 copy.62
  282.5 2.1 fusion.85
  284.5 0.6 dynamic-slice
  285.8 38.8 %all-reduce.12 = (f32[3,256]{1,0:T(4,128)S(1)}, f32[1024]{0:T(1024)S(1)}) all-reduce(f32[3,256]{1,0:T(4,128)S(1)} %get-tuple-element.60, f32[1024]{0:T(1024)S(1)} %get-tuple-element.58), channel_id=3, replica_groups=mesh['dp'=16,'tensor'=8] {'dp'}, use_global_device_ids=true, to_apply=%region_12.13.clone | all-reduce | flops 1792 | bytes 14336
  324.5 0.7 constant_dynamic-slice_fusion
  325.2 1.6 slice.97
  326.8 1.0 slice.96
  328.4 6.1 %convert_element_type.157 = bf16[1024,2048]{1,0:T(8,128)(2,1)} convert(f32[1024,2048]{1,0:T(8,128)} %get-tuple-element.16) | non-fusion elementwise | flops 2097152 | bytes 12582912 | tf_op jit(solution)/shard_map/convert_element_type | solution.py:619
  334.5 0.9 copy.55
  335.4 1.0 copy.56
  337.0 14.6 %reduce-scatter.5.cloned.1.call-done = f32[128,3]{1,0:T(8,128)} async-done(((f32[2048,3]{1,0:T(8,128)}), f32[128,3]{1,0:T(8,128)}) %reduce-scatter.5.cloned.1.call-update) | async-done | bytes 1552
  351.6 1.0 fusion.89
  352.7 0.6 copy.67
  353.3 0.6 copy.66
  354.4 7.9 %copy.72 = f32[1024,2048]{1,0:T(8,128)} copy(f32[1024,2048]{1,0:T(8,128)} %get-tuple-element.135) | data formatting | bytes 16777216
  (78 shorter events, 4.6 us)
Async XLA Ops:
  7.2 344.4 %reduce-scatter.5.cloned.1.call-start = ((), (), s32[]{:S(2)}) async-start(), calls=%async_computation.1 | async-start | bytes 1114112
  7.2 4.1 %copy-start.1 = (bf16[1024,2048]{1,0:T(8,128)(2,1)S(1)}, bf16[1024,2048]{1,0:T(8,128)(2,1)}, u32[]{:S(2)}) copy-start(bf16[1024,2048]{1,0:T(8,128)(2,1)} %x_ref.1) | copy-start | bytes 12582916
  8.2 4.4 %copy-start.9 = (bf16[2048]{0:T(1024)(128)(2,1)S(1)}, bf16[2048]{0:T(1024)(128)(2,1)}, u32[]{:S(2)}) copy-start(bf16[2048]{0:T(1024)(128)(2,1)} %param.13) | copy-start | bytes 12292
  8.2 4.4 %copy-start.10 = (bf16[2048]{0:T(1024)(128)(2,1)S(1)}, bf16[2048]{0:T(1024)(128)(2,1)}, u32[]{:S(2)}) copy-start(bf16[2048]{0:T(1024)(128)(2,1)} %param.14) | copy-start | bytes 12292
  12.6 2.1 copy-start.17
  14.7 19.4 %copy-start.2 = (bf16[1024,2048]{1,0:T(8,128)(2,1)}, bf16[1024,2048]{1,0:T(8,128)(2,1)S(1)}, u32[]{:S(2)}) copy-start(bf16[1024,2048]{1,0:T(8,128)(2,1)S(1)} %fusion.5.n_ref) | copy-start | bytes 12582916
  18.4 2.3 copy-start.3
  18.6 3.7 copy-start.18
  18.6 21.6 %copy-start.6 = (bf16[1024,4,32]{0,2,1:T(8,128)(2,1)}, bf16[1024,4,32]{0,2,1:T(8,128)(2,1)S(1)}, u32[]{:S(2)}) copy-start(bf16[1024,4,32]{0,2,1:T(8,128)(2,1)S(1)} %slice_bitcast_fusion.10) | copy-start | bytes 786436
  22.3 1.5 copy-start.4
  31.9 1.3 copy-start.14
  31.9 2.2 copy-start.16
  41.9 12.3 %copy-start = (f32[4,512,1024]{2,1,0:T(8,128)}, f32[4,512,1024]{2,1,0:T(8,128)S(1)}, u32[]{:S(2)}) copy-start(f32[4,512,1024]{2,1,0:T(8,128)S(1)} %get-tuple-element.89) | copy-start | bytes 25165828
  58.5 7.3 %copy-start.7 = (bf16[1024,4,32]{0,2,1:T(8,128)(2,1)S(1)}, bf16[1024,4,32]{0,2,1:T(8,128)(2,1)}, u32[]{:S(2)}) copy-start(bf16[1024,4,32]{0,2,1:T(8,128)(2,1)} %copy-done.6) | copy-start | bytes 786436
  67.2 0.9 copy-start.5
  68.3 1.0 copy-start.12
  68.3 1.7 copy-start.11
  68.6 0.7 copy-start.13
  84.5 196.6 %copy-start.8 = (f32[2048]{0:T(1024)S(1)}, f32[2048]{0:T(1024)}, u32[]{:S(2)}) copy-start(f32[2048]{0:T(1024)} %convert_reduce_fusion.1) | copy-start | bytes 24580
  254.4 30.2 %copy-start.19 = (u32[128]{0:T(128)S(1)}, u32[128]{0:T(128)}, u32[]{:S(2)}) copy-start(u32[128]{0:T(128)} %constant.56) | copy-start | bytes 1540
  352.7 9.6 %copy-start.15 = (f32[1,128]{1,0:T(1,128)}, f32[1,128]{1,0:T(1,128)S(1)}, u32[]{:S(2)}) copy-start(f32[1,128]{1,0:T(1,128)S(1)} %copy.68) | copy-start | bytes 1540
Sparse Core Ops, SparseCore 0:
  282.6 68.9 reduce-scatter.4
where the time goes:
time: 373 us; the launch traced here: 369 us
  Pallas kernels  170 us (46%)
  blocking collectives  64.6 us (17%)
  matrix products  46.4 us (12%)
  other arithmetic  32.5 us (9%)
  local copies, waits for them, and re-layouts  25.3 us (7%)
  between operations  16 us (4%)
  waiting for transfers between devices  14.6 us (4%)
    pallas_call x1, Pallas kernels, run_layer(): pl.pallas_call(layer_kernel, out_shape=(jax.ShapeDtypeStruct((LENGTH, D),...  170 us
    unnamed x1, blocking collectives  38.8 us
    psum x1, blocking collectives, per_device(): both = lax.psum(sums[:2], 'tensor')  25.8 us
    unnamed x50, local copies, waits for them, and re-layouts  15.8 us
    unnamed x2, waiting for transfers between devices  14.6 us
    dot_general x1, matrix products, per_device(): jnp.einsum('td,fd->tf', cotangent, shrink_weight, preferred_element_type=...  13 us
    convert_element_type x2, other arithmetic, per_device(): grad_scores = (chances * (grad_chances - row_dot)).astype(jnp.bfloat16)  8.89 us
    dot_general x2, matrix products, per_device(): jnp.einsum('sqhd,skhd->shqk', grad_rows, value_rows, preferred_element_ty...  7.61 us
  transfers between devices with their start and end apart: 1, of which 1 were waited for; matrix products, arithmetic and copies ran while one was open for 4% of the time, Pallas kernels for 0%

commit v1 on v0

v1 whole, which is shorter than its diff:
```python
import jax
import jax.numpy as jnp
import numpy as np
from jax import lax
from jax.experimental import pallas as pl
from jax.experimental.pallas import tpu as pltpu
from jax.sharding import PartitionSpec as P

HD = 64
ROT = 32
LENGTH = 1024
D = 2048
F32 = jnp.float32
BF16 = jnp.bfloat16
MESH = pl.DeviceIdType.MESH

rotary_base = 10000.0
norm_eps = 1e-05

CH = 256
UNITS = 16
UROWS = 128
BATCHES = 16
BROWS = 192
KX = 5
KY = 5
KZ = 5
KT = 8
KG = 4
TICKS = 23


def gelu_parts(v):
    th = jnp.tanh(0.7978845608 * (v + 0.044715 * v * v * v))
    return th, 0.5 * (1.0 + th)


def layer_kernel(
    x_hbm, g_hbm, sw_hbm, dw_hbm, ew_hbm, aw_hbm, cos_hbm, sin_hbm, gain_hbm, shift_hbm, eb_hbm, ab_hbm, db_hbm, sb_hbm,
    all_ref, f_ref, small_ref,
    vec_ref, gain_ref, shift_ref, eb_ref, ab_ref, db_ref, sb_ref, xo_ref, g_ref, n_ref, act_ref, att_ref, gh_ref, gp_ref, q_ref, k_ref, v_ref, ga_ref,
    st_ref, top_ref, sum_ref, dq_ref, dk_ref, dv_ref, km_ref, qm_ref, gm_ref, pm_ref, dl_ref, ds_ref, cos_ref, sin_ref, sw_ref, dw_ref, ew_ref, aw_ref, gs_ref,
    va, vb, vc, vd, ve,
    stream, turned, part, core_in, mine, zp, zd, zb, zg, done,
    xp, xd, xb, mid, yp, yd, yb,
    xsend, xrecv, ysend, yrecv, csend, crecv, zsend, zrecv, gsend, grecv, ssend, srecv, lsem,
    isem, osem, vsend, vrecv,
):
    dp = lax.axis_index("dp")
    tn = lax.axis_index("tensor")
    x, y, c, z = dp % 4, dp // 4, tn % 2, tn // 2

    def side(axis, sg):
        if axis == 0:
            return (y * 4 + (x + sg + 4) % 4, tn)
        if axis == 1:
            return (((y + sg + 4) % 4) * 4 + x, tn)
        if axis == 2:
            return (dp, ((z + sg + 4) % 4) * 2 + c)
        return (dp, z * 2 + 1 - c)

    def load(k):
        rows = pl.ds((k % 4) * CH, CH)
        src, dst = (
            (x_hbm.at[rows], n_ref.at[rows])
            if k < 4
            else (g_hbm.at[rows], g_ref.at[rows])
            if k < 8
            else (
                (sw_hbm, sw_ref),
                (dw_hbm, dw_ref),
                (ew_hbm, ew_ref),
                (aw_hbm, aw_ref),
                (cos_hbm, cos_ref),
                (sin_hbm, sin_ref),
                (gain_hbm, gain_ref),
                (shift_hbm, shift_ref),
                (db_hbm, db_ref),
                (sb_hbm, sb_ref),
                (eb_hbm, eb_ref),
                (ab_hbm, ab_ref),
            )[k - 8]
        )
        return pltpu.make_async_copy(src, dst, isem.at[k])

    for k in (0, 14, 15, 16, 17, 18, 19, 10, 11):
        load(k).start()

    SIDES = [(0, 1), (0, -1), (0, 2), (1, 1), (1, -1), (1, 2), (2, 1), (2, -1), (2, 2), (3, 0)]
    barrier = pltpu.get_barrier_semaphore()
    for axis, sg in SIDES:
        pl.semaphore_signal(barrier, inc=1, device_id=side(axis, sg), device_id_type=MESH)

    gs_ref[...] = jnp.zeros_like(gs_ref)

    def remote(src, dst, ssem, rsem, to):
        return pltpu.make_async_remote_copy(
            src_ref=src, dst_ref=dst, send_sem=ssem, recv_sem=rsem, device_id=to, device_id_type=MESH
        )

    def within(i, n):
        return (i >= 0) & (i < n)

    def when(cond, body, *args):
        pl.when(cond)(lambda: body(*args))

    NT = (((1,), (1,)), ((), ()))
    SG = (1, -1)
    HALVES = (0, 1)

    def rows_of(b, h, hh):
        return pl.ds(pl.multiple_of((b % 4) * BROWS + h * 96 + hh * 48, 8), 48)

    def own_rows(b, h, piece, hh):
        return (
            stream.at[:, piece, rows_of(b, h, hh)]
            if h == 0
            else stream.at[piece, :, rows_of(b, h, hh)]
        )

    def first(kind, h, d, b):
        a = (x, y)[h]
        sg = SG[d]
        slot = b % KX
        sems = (xsend.at[kind, h, d, slot], xrecv.at[kind, h, d, slot], side(h, sg))
        if kind == 0:
            return remote(own_rows(b, h, (a + 2) % 4, d), xp.at[h, d, slot], *sems)
        if kind == 1:
            return remote(own_rows(b, h, (a + sg + 4) % 4, 1 - d), xd.at[h, d, slot], *sems)
        return remote(xp.at[h, d, slot], xb.at[h, d, slot], *sems)

    def second(kind, h, d, b):
        a = (y, x)[h]
        sg = SG[d]
        slot = b % KY
        sems = (ysend.at[kind, h, d, slot], yrecv.at[kind, h, d, slot], side(1 - h, sg))
        if kind == 0:
            return remote(mid.at[h, b % 3, (a + 2) % 4, pl.ds(d * 48, 48)], yp.at[h, d, slot], *sems)
        if kind == 1:
            return remote(
                mid.at[h, b % 3, (a + sg + 4) % 4, pl.ds((1 - d) * 48, 48)], yd.at[h, d, slot], *sems
            )
        return remote(yp.at[h, d, slot], yb.at[h, d, slot], *sems)

    def each(make, kinds, b):
        for kind in kinds:
            for h in HALVES:
                for d in (0, 1):
                    yield make(kind, h, d, b)

    def x0(b):
        for copy in each(first, (0, 1), b):
            copy.start()

    def x1(b):
        slot = b % KX
        for h in HALVES:
            for d in (0, 1):
                a = (x, y)[h]
                first(0, h, d, b).wait_recv()
                xp[h, d, slot] = xp[h, d, slot] + own_rows(b, h, (a + SG[d] + 4) % 4, d)[...]
                first(2, h, d, b).start()

    def x2(b):
        slot = b % KX
        for h in HALVES:
            a = (x, y)[h]
            for d in (0, 1):
                first(1, h, d, b).wait_recv()
                first(2, h, d, b).wait_recv()
            for hh in (0, 1):
                mid[h, b % 3, :, pl.ds(hh * 48, 48)] = (
                    own_rows(b, h, a, hh)[...] + xb[h, hh, slot] + xd[h, 1 - hh, slot]
                )
            for kind in (0, 1):
                for d in (0, 1):
                    second(kind, h, d, b).start()
        for copy in each(first, (0, 1, 2), b):
            copy.wait_send()

    def x3(b):
        slot = b % KY
        for h in HALVES:
            a = (y, x)[h]
            for d in (0, 1):
                second(0, h, d, b).wait_recv()
                yp[h, d, slot] = (
                    yp[h, d, slot] + mid[h, b % 3, (a + SG[d] + 4) % 4, pl.ds(d * 48, 48)]
                )
                second(2, h, d, b).start()

    def x4(b):
        slot = b % KY
        for h in HALVES:
            a = (y, x)[h]
            for d in (0, 1):
                second(1, h, d, b).wait_recv()
                second(2, h, d, b).wait_recv()
            for hh in (0, 1):
                at = pl.ds(pl.multiple_of(b * BROWS + h * 96 + hh * 48, 8), 48)
                f_ref[at] = mid[h, b % 3, a, pl.ds(hh * 48, 48)] + yb[h, hh, slot] + yd[h, 1 - hh, slot]
        for copy in each(second, (0, 1, 2), b):
            copy.wait_send()

    def zrows(u, piece, hh):
        return mine.at[u % 3, pl.ds(pl.multiple_of(piece * 16 + hh * 8, 8), 8)]

    def along(kind, d, u):
        sg = SG[d]
        slot = u % KZ
        sems = (zsend.at[kind, d, slot], zrecv.at[kind, d, slot], side(2, sg))
        if kind == 0:
            return remote(zrows(u, (z + 2) % 4, d), zp.at[d, slot], *sems)
        if kind == 1:
            return remote(zrows(u, (z + sg + 4) % 4, 1 - d), zd.at[d, slot], *sems)
        return remote(zp.at[d, slot], zb.at[d, slot], *sems)

    def cross(u):
        return remote(
            part.at[u % 2, pl.ds(pl.multiple_of((1 - c) * 64, 64), 64)],
            core_in.at[u % 2],
            csend.at[u % 2],
            crecv.at[u % 2],
            side(3, 0),
        )

    def grow(u, cc, piece, off, size):
        return pl.ds(pl.multiple_of((u % 8) * UROWS + cc * 64 + piece * 16 + off, 8), size)

    def gather1(d, u):
        slot = u % KZ
        return remote(
            done.at[u % 2], zg.at[u % KG, d], gsend.at[0, d, slot], grecv.at[0, d, slot],
            side(2, SG[d]),
        )

    def gather2(d, u):
        slot = u % KZ
        half = pl.ds(d * 8, 8)
        return remote(
            zg.at[u % KG, d, half], zg.at[u % KG, 2, half], gsend.at[1, d, slot],
            grecv.at[1, d, slot], side(2, SG[d]),
        )

    def block_rows(k, u):
        return all_ref.at[u // 8, grow(u, c, (z + (0, -1, 1, 2)[k] + 4) % 4, 0, 16)]

    def block_held(k, u):
        return done.at[u % 2] if k == 0 else zg.at[u % KG, k - 1]

    def twin(k, u):
        slot = u % KT
        return remote(
            block_held(k, u), block_rows(k, u), ssend.at[k, slot], srecv.at[k, slot], side(3, 0)
        )

    def keep(k, u):
        return pltpu.make_async_copy(block_held(k, u), block_rows(k, u), lsem.at[k, u % KG])

    def partial(u, j):
        rows = pl.ds(pl.multiple_of((u % 8) * UROWS, CH), CH)
        cols = pl.ds(pl.multiple_of(j * 1024, 1024), 1024)

        def put(total):
            part[0, :, cols] = total[:UROWS]
            part[1, :, cols] = total[UROWS:]

        @pl.when(u < 8)
        def _():
            put(
                jnp.dot(act_ref[rows, :], sw_ref[:, cols], preferred_element_type=F32)
                + jnp.dot(att_ref[rows, :], dw_ref[:, cols], preferred_element_type=F32)
            )

        @pl.when(u >= 8)
        def _():
            total = lax.dot_general(
                gh_ref[rows, :], ew_ref[cols, :], NT, preferred_element_type=F32
            )
            for k in range(3):
                total += lax.dot_general(
                    gp_ref[k, rows, :], aw_ref[k, cols, :], NT, preferred_element_type=F32
                )
            put(total)

    def z1(u):
        cross(u).wait_recv()

        @pl.loop(0, 2)
        def _(k):
            at = pl.ds(pl.multiple_of(k * 32, 32), 32)
            mine[u % 3, at] = (
                part[u % 2, pl.ds(pl.multiple_of(c * 64 + k * 32, 32), 32)] + core_in[u % 2, at]
            )

        for kind in (0, 1):
            for d in (0, 1):
                along(kind, d, u).start()
        cross(u).wait_send()

    def own_x(u):
        rows = pl.ds(pl.multiple_of((u % 8) * UROWS + c * 64 + z * 16, 16), 16)
        return pltpu.make_async_copy(x_hbm.at[rows], xo_ref.at[u % 2], osem.at[u % 2])

    def z2(u):
        slot = u % KZ
        own_x(u).start()
        for d in (0, 1):
            along(0, d, u).wait_recv()
            zp[d, slot] = zp[d, slot] + zrows(u, (z + SG[d] + 4) % 4, d)[...]
            along(2, d, u).start()

    def z3(u):
        slot = u % KZ
        for d in (0, 1):
            along(1, d, u).wait_recv()
            along(2, d, u).wait_recv()
        whole = jnp.concatenate(
            [zrows(u, z, hh)[...] + zb[hh, slot] + zd[1 - hh, slot] for hh in (0, 1)], axis=0
        )
        rows = pl.ds(pl.multiple_of((u % 8) * UROWS + c * 64 + z * 16, 16), 16)
        own_x(u).wait()
        states = xo_ref[u % 2].astype(F32)

        @pl.when(u < 8)
        def _():
            done[u % 2] = states + whole + vec_ref[2:3, :]

        @pl.when(u >= 8)
        def _():
            center = jnp.mean(states, axis=-1, keepdims=True)
            centred = states - center
            spread = jnp.mean(centred * centred, axis=-1, keepdims=True)
            r = lax.rsqrt(spread + norm_eps)
            zz = centred * r
            e = whole * vec_ref[0:1, :]
            done[u % 2] = g_ref[rows, :].astype(F32) + r * (
                e
                - jnp.mean(e, axis=-1, keepdims=True)
                - zz * jnp.mean(e * zz, axis=-1, keepdims=True)
            )
            gs_ref[0:1, :] += jnp.sum(whole * zz, axis=0, keepdims=True)
            gs_ref[1:2, :] += jnp.sum(whole, axis=0, keepdims=True)

        for d in (0, 1):
            gather1(d, u).start()
        twin(0, u).start()
        keep(0, u).start()
        for kind in (0, 1, 2):
            for d in (0, 1):
                along(kind, d, u).wait_send()

    def z4(u):
        for d in (0, 1):
            gather1(d, u).wait_recv()
        for d in (0, 1):
            gather2(d, u).start()
        for d in (0, 1):
            twin(1 + d, u).start()
            keep(1 + d, u).start()
        keep(0, u).wait()
        for d in (0, 1):
            gather1(d, u).wait_send()
        twin(0, u).wait_send()

    def z5(u):
        for d in (0, 1):
            gather2(d, u).wait_recv()
        twin(3, u).start()
        keep(3, u).start()
        for d in (0, 1):
            gather2(d, u).wait_send()
            twin(1 + d, u).wait_send()
            keep(1 + d, u).wait()

    def z6(u):
        twin(3, u).wait_send()
        keep(3, u).wait()
        for k in range(4):
            twin(k, u).wait_recv()

    def product(left, right, j, q):
        @pl.when(q == 0)
        def _():
            turned[...] = left[...].T

        at = pl.ds(pl.multiple_of((j % 3) * 256, 256), 256)
        both = jnp.dot(
            turned[...],
            right[:, pl.ds(pl.multiple_of(q * 1024, 1024), 1024)],
            preferred_element_type=F32,
        )
        for k in range(8):
            stream[q * 2 + k // 4, k % 4, at] = both[:, k * 128 : (k + 1) * 128]

    def block(j, q):
        cols = pl.ds(pl.multiple_of(j % 4 * 256, 256), 256)
        when(j < 4, product, act_ref.at[:, cols], g_ref, j, q)
        when((j >= 4) & (j < 8), product, gh_ref.at[:, cols], n_ref, j, q)
        when(j == 8, product, att_ref, g_ref, j, q)
        when(j > 8, product, gp_ref.at[jnp.maximum(j - 9, 0)], n_ref, j, q)

    lane = lax.broadcasted_iota(jnp.int32, (1, 256), 1)

    def chunk(i):
        return pl.ds(pl.multiple_of(i * CH, CH), CH)

    def norm_chunk(i):
        @pl.loop(0, 2)
        def _(k):
            rows = pl.ds(pl.multiple_of(i * CH + k * 128, 128), 128)
            states = n_ref[rows, :].astype(F32)
            centred = states - jnp.mean(states, axis=-1, keepdims=True)
            spread = jnp.mean(centred * centred, axis=-1, keepdims=True)
            n_ref[rows, :] = (
                centred * lax.rsqrt(spread + norm_eps) * vec_ref[0:1, :] + vec_ref[1:2, :]
            ).astype(BF16)

    def expand_part(rows, j):
        cols = pl.ds(pl.multiple_of(j * 256, 256), 256)
        hidden = (
            jnp.dot(n_ref[rows, :], ew_ref[:, cols], preferred_element_type=F32)
            + vec_ref[3:4, cols]
        )
        th, half = gelu_parts(hidden)
        act_ref[rows, cols] = (hidden * half).astype(BF16)
        gh_ref[rows, cols] = (
            half
            + (0.5 * 0.7978845608) * hidden * (1.0 - th * th) * (
                1.0 + (3 * 0.044715) * hidden * hidden
            )
        ).astype(BF16)

    def hidden_back(j):
        cols = pl.ds(pl.multiple_of(j * 256, 256), 256)
        back = lax.dot_general(g_ref[...], sw_ref[cols, :], NT, preferred_element_type=F32)
        gh_ref[:, cols] = (back * gh_ref[:, cols].astype(F32)).astype(BF16)

    def turn(values, i, way):
        cosine = cos_ref[chunk(i), :]
        sine = sin_ref[chunk(i), :] * way
        low = lax.broadcasted_iota(jnp.int32, (1, 128), 1) % HD < ROT // 2
        halves = []
        for k in (0, 1):
            v = values[:, k * 128 : (k + 1) * 128]
            swapped = jnp.where(low, -pltpu.roll(v, 128 - ROT // 2, 1), pltpu.roll(v, ROT // 2, 1))
            halves.append(v * cosine + swapped * sine)
        return jnp.concatenate(halves, axis=1)

    def project_chunk(i):
        rows = chunk(i)

        def proj(k):
            return (
                jnp.dot(n_ref[rows, :], aw_ref[k], preferred_element_type=F32)
                + vec_ref[4:5, k * 256 : (k + 1) * 256]
            )

        q_ref[rows, :] = (turn(proj(0), i, 1.0).astype(BF16).astype(F32) * HD**-0.5).astype(BF16)
        k_ref[rows, :] = turn(proj(1), i, 1.0).astype(BF16)
        v_ref[rows, :] = proj(2).astype(BF16)
        ga_ref[rows, :] = lax.dot_general(
            g_ref[rows, :], dw_ref[...], NT, preferred_element_type=F32
        ).astype(BF16)

    HEADS = [slice(h * CH, (h + 1) * CH) for h in range(4)]
    high = lax.broadcasted_iota(jnp.int32, (256, 1), 0)

    def stack_heads(out, values):
        for h in range(4):
            out[HEADS[h], :] = jnp.where(lane // HD == h, values, 0)

    def scores_of(i, j, h, scores):
        allowed = j * CH + lax.broadcasted_iota(
            jnp.int32, (CH, CH), 0
        ) <= i * CH + lax.broadcasted_iota(jnp.int32, (CH, CH), 1)
        return jnp.where(allowed, scores[:, HEADS[h]], -1e30)

    def scores_pair(i, j):
        return lax.dot_general(k_ref[chunk(j), :], qm_ref[...], NT, preferred_element_type=F32)

    def attend_begin(i):
        stack_heads(qm_ref, q_ref[chunk(i), :])
        top_ref[...] = jnp.full_like(top_ref, -1e30)
        sum_ref[...] = jnp.zeros_like(sum_ref)
        dk_ref[...] = jnp.zeros_like(dk_ref)

    def attend_pair(i, j):
        rows = chunk(i)
        scores = scores_pair(i, j)
        values_turned = v_ref[chunk(j), :].T
        for h in range(4):
            part_scores = scores_of(i, j, h, scores)
            old = top_ref[h : h + 1, :]
            top = jnp.maximum(old, jnp.max(part_scores, axis=0, keepdims=True))
            less = jnp.exp(old - top)
            expo = jnp.exp(part_scores - top)
            sum_ref[h : h + 1, :] = sum_ref[h : h + 1, :] * less + jnp.sum(
                expo, axis=0, keepdims=True
            )
            top_ref[h : h + 1, :] = top
            km_ref[:, HEADS[h]] = jnp.where(high // HD == h, values_turned, 0)
            ds_ref[HEADS[h], :] = expo.astype(BF16)
            dk_ref[h * HD : (h + 1) * HD, :] = dk_ref[h * HD : (h + 1) * HD, :] * less
        dk_ref[...] += jnp.dot(km_ref[...], ds_ref[...], preferred_element_type=F32)

        @pl.when(j == i)
        def _():
            for h in range(4):
                at = slice(h * HD, (h + 1) * HD)
                dk_ref[at, :] = dk_ref[at, :] * (1.0 / sum_ref[h : h + 1, :])
            st_ref[0:4, rows] = top_ref[0:4, :] + jnp.log(sum_ref[0:4, :])
            total = dk_ref[...]
            att_ref[rows, :] = total.T.astype(BF16)
            dots = total * ga_ref[rows, :].astype(F32).T
            for h in range(4):
                st_ref[4 + h : 5 + h, rows] = jnp.sum(
                    dots[h * HD : (h + 1) * HD], axis=0, keepdims=True
                )

    def attend_back(j, i):
        rows = chunk(j)
        qrows = chunk(i)
        key = k_ref[rows, :]

        @pl.when(i == j)
        def _():
            keys_turned = key.T
            for h in range(4):
                km_ref[:, HEADS[h]] = jnp.where(high // HD == h, keys_turned, 0)
            dk_ref[...] = jnp.zeros_like(dk_ref)
            dv_ref[...] = jnp.zeros_like(dv_ref)

        stack_heads(qm_ref, q_ref[qrows, :])
        stack_heads(gm_ref, ga_ref[qrows, :])
        scores = lax.dot_general(key, qm_ref[...], NT, preferred_element_type=F32)
        back = lax.dot_general(v_ref[rows, :], gm_ref[...], NT, preferred_element_type=F32)
        for h in range(4):
            chances = jnp.exp(scores_of(i, j, h, scores) - st_ref[h : h + 1, qrows])
            dscore = (chances * (back[:, HEADS[h]] - st_ref[4 + h : 5 + h, qrows])).astype(BF16)
            pm_ref[:, HEADS[h]] = chances.astype(BF16)
            dl_ref[:, HEADS[h]] = dscore
            ds_ref[HEADS[h], :] = dscore
        dk_ref[...] += jnp.dot(dl_ref[...], qm_ref[...], preferred_element_type=F32)
        dv_ref[...] += jnp.dot(pm_ref[...], gm_ref[...], preferred_element_type=F32)
        dq_ref[:, qrows] += jnp.dot(km_ref[...], ds_ref[...], preferred_element_type=F32)

        @pl.when(i == 3)
        def _():
            gp_ref[0, rows, :] = turn(dq_ref[:, rows].T * HD**-0.5, j, -1.0).astype(BF16)
            gp_ref[1, rows, :] = turn(dk_ref[...], j, -1.0).astype(BF16)
            gp_ref[2, rows, :] = dv_ref[...].astype(BF16)

    def token_sums():
        ones = jnp.ones((8, LENGTH), BF16)
        sums = jnp.dot(ones, g_ref[...], preferred_element_type=F32)
        hsum = jnp.dot(ones, gh_ref[...], preferred_element_type=F32)
        psum = [jnp.dot(ones, gp_ref[k], preferred_element_type=F32) for k in range(3)]
        for p in range(16):
            vc[p // 4, p % 4, 2:3] = sums[0:1, p * 128 : (p + 1) * 128]
            vc[p // 4, p % 4, 3:4] = hsum[0:1, p // 2 * 128 : (p // 2 + 1) * 128]
            for k in range(3):
                vc[p // 4, p % 4, 4 + k : 5 + k] = psum[k][0:1, p // 8 * 128 : (p // 8 + 1) * 128]
            vc[p // 4, p % 4, 7:8] = jnp.zeros((1, 128), F32)

    def v_core():
        return remote(va, vb.at[3], vsend.at[0], vrecv.at[0], side(3, 0))

    def v_z(k):
        return remote(va, vb.at[k], vsend.at[1 + k], vrecv.at[1 + k], side(2, (1, -1, 2)[k]))

    def v_x(k):
        sg = (1, -1, 2)[k]
        return remote(vc.at[:, (x + sg + 4) % 4], vd.at[k], vsend.at[4 + k], vrecv.at[4 + k], side(0, sg))

    def v_y(k):
        sg = (1, -1, 2)[k]
        return remote(vd.at[3, (y + sg + 4) % 4], ve.at[k], vsend.at[7 + k], vrecv.at[7 + k], side(1, sg))

    def v0():
        for p in range(16):
            va[p : p + 1] = gs_ref[0:1, p * 128 : (p + 1) * 128]
            va[16 + p : 17 + p] = gs_ref[1:2, p * 128 : (p + 1) * 128]
        v_core().start()

    def v1():
        v_core().wait()
        va[...] = va[...] + vb[3]
        for k in range(3):
            v_z(k).start()

    def v2():
        for k in range(3):
            v_z(k).wait()
        both = va[...] + vb[0] + vb[1] + vb[2]
        for p in range(16):
            vc[p // 4, p % 4, 0:1] = both[p : p + 1]
            vc[p // 4, p % 4, 1:2] = both[16 + p : 17 + p]
        for k in range(3):
            v_x(k).start()

    def v3():
        for k in range(3):
            v_x(k).wait()
        vd[3] = vc[:, x] + vd[0] + vd[1] + vd[2]
        for k in range(3):
            v_y(k).start()

    def v4():
        for k in range(3):
            v_y(k).wait()
        total = vd[3, y] + ve[0] + ve[1] + ve[2]
        small_ref[...] = total
        small_ref[3:4, 0:64] = jnp.where(dp % 2 == 0, total[3:4, 0:64], total[3:4, 64:128])
        mine_of = jnp.zeros((3, 16), F32)
        for k in range(8):
            mine_of = jnp.where(dp % 8 == k, total[4:7, k * 16 : (k + 1) * 16], mine_of)
        small_ref[4:7, 0:16] = mine_of

    def attend_item(k):
        i = at_least(k, 2) + at_least(k, 5) + at_least(k, 9)
        r = k - i * (i + 3) // 2

        @pl.when(r == 0)
        def _():
            project_chunk(i)
            attend_begin(i)

        when(r > 0, attend_pair, i, r - 1)

    def back_item(k):
        j = at_least(k, 4) + at_least(k, 7) + at_least(k, 9)
        attend_back(j, j + k - j * (9 - j) // 2)

    def at_least(k, bound):
        return jnp.where(k >= bound, 1, 0)

    def between(h, first, last):
        return (h >= first) & (h <= last)

    def stage(t, late, body):
        when((t >= late) & (t < late + 16), body, t - late)

    dq_ref[...] = jnp.zeros_like(dq_ref)
    for k in range(14, 20):
        load(k).wait()
    vec_ref[0:1, :] = gain_ref[...].astype(F32).reshape(1, D)
    vec_ref[1:2, :] = shift_ref[...].astype(F32).reshape(1, D)
    vec_ref[2:3, :] = (db_ref[...].astype(F32) + sb_ref[...].astype(F32)).reshape(1, D)
    vec_ref[3:4, 0:1024] = eb_ref[...].astype(F32).reshape(1, 1024)
    for k in range(3):
        vec_ref[4:5, k * 256 : (k + 1) * 256] = ab_ref[k : k + 1, :].astype(F32)
    pl.semaphore_wait(barrier, len(SIDES))

    @pl.loop(0, TICKS)
    def _(t):
        @pl.loop(0, 4)
        def _(pos):
            h = t * 4 + pos

            @pl.when(pos == 0)
            def _():
                stage(t, 6, z5)
                stage(t, 1, z1)
                stage(t, 7, x4)
                stage(t, 2, x0)
                when(t == 19, v1)
                when(t == 20, v3)

            @pl.when(pos == 1)
            def _():
                stage(t, 7, z6)
                stage(t, 2, z2)
                stage(t, 3, x1)

            @pl.when(pos == 2)
            def _():
                stage(t, 3, z3)
                stage(t, 4, x2)
                when(t == 18, v0)
                when(t == 19, v2)
                when(t == 20, v4)

            @pl.when(pos == 3)
            def _():
                stage(t, 4, z4)
                stage(t, 5, x3)

            @pl.when(t < UNITS)
            def _():
                when((pos > 0) & (pos < 3) & (t % 2 == 0), partial, t, pos - 1)
                when(pos == 2, lambda: cross(t).start())
                w = t - 1
                when(
                    (pos >= 2) & (w >= 0) & (w % 4 < 3),
                    lambda: block(w // 4 * 3 + w % 4, pos - 2),
                )

                @pl.when(h < 4)
                def _():
                    @pl.when(h == 0)
                    def _():
                        load(0).wait()
                        for k in (12, 13, 4, 9, 8):
                            load(k).start()

                    for k in range(1, 4):
                        when(h == k, load(k).wait)
                    norm_chunk(h)

                @pl.when(h == 0)
                def _():
                    load(10).wait()
                    pl.loop(0, 4)(lambda j: expand_part(pl.ds(0, CH), j))
                    for k in (1, 2, 3, 5, 6, 7):
                        load(k).start()
                    for k in (4, 9, 11, 12, 13):
                        load(k).wait()

                @pl.when(h == 3)
                def _():
                    for k in (5, 6, 7):
                        load(k).wait()

                first = jnp.where(h <= 3, 0, jnp.where(h <= 5, 1, 3))
                pl.loop(
                    first,
                    first + jnp.where(h == 5, 2, jnp.where((h == 3) | (h == 7), 1, 0)),
                )(lambda j: expand_part(pl.ds(CH, LENGTH - CH), j))
                first = jnp.where(h <= 2, 0, jnp.where(h == 3, 2, jnp.where(h <= 4, 4, h - 2)))
                pl.loop(
                    first,
                    first
                    + jnp.where(
                        (h == 0) | (h == 3), 2, jnp.where((h == 4) | between(h, 7, 15), 1, 0)
                    ),
                )(attend_item)
                when(between(h, 18, 19) | between(h, 23, 24), hidden_back, jnp.where(h < 20, h - 18, h - 21))
                back = jnp.where(
                    h <= 30, h - 27, jnp.where(h <= 36, h - 30, jnp.where(h <= 43, h - 35, 9))
                )
                when(
                    between(h, 27, 30) | between(h, 34, 36) | between(h, 42, 43) | (h == 53),
                    back_item,
                    back,
                )
                when(h == 54, token_sums)
                when(h == 0, load(8).wait)


def rotary_tables():
    freqs = np.exp(
        -np.arange(ROT // 2).astype(np.float32) * np.float32(2.0 / ROT) * np.log(np.float32(rotary_base))
    ).astype(np.float32)
    angles = np.arange(LENGTH).astype(np.float32)[:, None] * freqs[None, :]
    rest = np.zeros((LENGTH, HD - ROT), np.float32)
    one = np.concatenate([np.cos(angles), np.cos(angles), rest + 1], axis=1)
    two = np.concatenate([np.sin(angles), np.sin(angles), rest], axis=1)
    return (
        np.tile(one, (1, 2)).astype(np.float32),
        np.tile(two, (1, 2)).astype(np.float32),
    )


def run_layer(x, g, sw, dw, ew, aw, *vectors):
    vmem = pl.BlockSpec(memory_space=pltpu.VMEM)
    anym = pl.BlockSpec(memory_space=pl.ANY)
    dma = pltpu.SemaphoreType.DMA
    cosine, sine = rotary_tables()
    return pl.pallas_call(
        layer_kernel,
        out_shape=(
            jax.ShapeDtypeStruct((2, LENGTH, D), F32),
            jax.ShapeDtypeStruct((3072, 128), F32),
            jax.ShapeDtypeStruct((8, 128), F32),
        ),
        in_specs=[anym] * 14,
        out_specs=(anym, vmem, vmem),
        scratch_shapes=[
            pltpu.VMEM((8, D), F32),
            pltpu.VMEM((D,), BF16),
            pltpu.VMEM((D,), BF16),
            pltpu.VMEM((1024,), BF16),
            pltpu.VMEM((3, 256), BF16),
            pltpu.VMEM((D,), BF16),
            pltpu.VMEM((D,), BF16),
            pltpu.VMEM((2, 16, D), BF16),
            pltpu.VMEM((LENGTH, D), BF16),
            pltpu.VMEM((LENGTH, D), BF16),
            pltpu.VMEM((LENGTH, 1024), BF16),
            pltpu.VMEM((LENGTH, 256), BF16),
            pltpu.VMEM((LENGTH, 1024), BF16),
            pltpu.VMEM((3, LENGTH, 256), BF16),
            pltpu.VMEM((LENGTH, 256), BF16),
            pltpu.VMEM((LENGTH, 256), BF16),
            pltpu.VMEM((LENGTH, 256), BF16),
            pltpu.VMEM((LENGTH, 256), BF16),
            pltpu.VMEM((8, LENGTH), F32),
            pltpu.VMEM((8, CH), F32),
            pltpu.VMEM((8, CH), F32),
            pltpu.VMEM((256, LENGTH), F32),
            pltpu.VMEM((CH, 256), F32),
            pltpu.VMEM((CH, 256), F32),
            pltpu.VMEM((256, 4 * CH), BF16),
            pltpu.VMEM((4 * CH, 256), BF16),
            pltpu.VMEM((4 * CH, 256), BF16),
            pltpu.VMEM((CH, 4 * CH), BF16),
            pltpu.VMEM((CH, 4 * CH), BF16),
            pltpu.VMEM((4 * CH, CH), BF16),
            pltpu.VMEM((LENGTH, 128), F32),
            pltpu.VMEM((LENGTH, 128), F32),
            pltpu.VMEM((1024, D), BF16),
            pltpu.VMEM((256, D), BF16),
            pltpu.VMEM((D, 1024), BF16),
            pltpu.VMEM((3, D, 256), BF16),
            pltpu.VMEM((8, D), F32),
            pltpu.VMEM((32, 128), F32),
            pltpu.VMEM((4, 32, 128), F32),
            pltpu.VMEM((4, 4, 8, 128), F32),
            pltpu.VMEM((4, 4, 8, 128), F32),
            pltpu.VMEM((3, 8, 128), F32),
            pltpu.VMEM((4, 4, 4 * BROWS, 128), F32),
            pltpu.VMEM((256, LENGTH), BF16),
            pltpu.VMEM((2, UROWS, D), F32),
            pltpu.VMEM((2, 64, D), F32),
            pltpu.VMEM((3, 64, D), F32),
            pltpu.VMEM((2, KZ, 8, D), F32),
            pltpu.VMEM((2, KZ, 8, D), F32),
            pltpu.VMEM((2, KZ, 8, D), F32),
            pltpu.VMEM((KG, 3, 16, D), F32),
            pltpu.VMEM((2, 16, D), F32),
            pltpu.VMEM((2, 2, KX, 4, 48, 128), F32),
            pltpu.VMEM((2, 2, KX, 4, 48, 128), F32),
            pltpu.VMEM((2, 2, KX, 4, 48, 128), F32),
            pltpu.VMEM((2, 3, 4, 96, 128), F32),
            pltpu.VMEM((2, 2, KY, 48, 128), F32),
            pltpu.VMEM((2, 2, KY, 48, 128), F32),
            pltpu.VMEM((2, 2, KY, 48, 128), F32),
            dma((3, 2, 2, KX)),
            dma((3, 2, 2, KX)),
            dma((3, 2, 2, KY)),
            dma((3, 2, 2, KY)),
            dma((2,)),
            dma((2,)),
            dma((3, 2, KZ)),
            dma((3, 2, KZ)),
            dma((2, 2, KZ)),
            dma((2, 2, KZ)),
            dma((4, KT)),
            dma((4, KT)),
            dma((4, KG)),
            dma((20,)),
            dma((2,)),
            dma((10,)),
            dma((10,)),
        ],
        compiler_params=pltpu.CompilerParams(
            collective_id=0, has_side_effects=True, vmem_limit_bytes=62 << 20
        ),
        cost_estimate=pl.CostEstimate(flops=20 << 30, bytes_accessed=60 << 20, transcendentals=0),
    )(x, g, sw, dw, ew, aw, jnp.asarray(cosine), jnp.asarray(sine), *vectors)


def finish_kernel(
    go_ref, gi_ref, f_ref, small_ref,
    out_ref, grad_ref, gain_ref, shift_ref, attn_ref, ab_ref, dense_ref, db_ref,
    expand_ref, eb_ref, shrink_ref, sb_ref,
):
    out_ref[...] = go_ref[0].astype(BF16)
    grad_ref[...] = gi_ref[0]

    @pl.when(pl.program_id(0) == 0)
    def _():
        gain_ref[...] = small_ref[0:1, :].reshape(128)
        shift_ref[...] = small_ref[1:2, :].reshape(128)
        db_ref[...] = small_ref[2:3, :].reshape(128)
        sb_ref[...] = small_ref[2:3, :].reshape(128)
        eb_ref[...] = small_ref[3:4, 0:64].reshape(64)
        ab_ref[...] = small_ref[4:7, 0:16]
        shrink_ref[...] = f_ref[0:1024]
        dense_ref[...] = f_ref[2048:2304]
        for k in range(8):
            expand_ref[:, k * 128 : (k + 1) * 128] = f_ref[1024 + k * 128 : 1152 + k * 128].T
        for k in range(6):
            attn_ref[k // 2, :, k % 2 * 128 : (k % 2 + 1) * 128] = (
                f_ref[2304 + k * 128 : 2432 + k * 128].T
            )


def finish(both, pieces, small):
    def whole(*shape):
        return pl.BlockSpec(shape, lambda i: (0,) * len(shape))

    def f32(*shape):
        return jax.ShapeDtypeStruct(shape, F32)

    spec = pl.BlockSpec((512, D), lambda i: (i, 0))
    shapes = (
        (128,), (128,), (3, 128, 256), (3, 16), (256, 128), (128,), (128, 1024), (64,), (1024, 128),
        (128,),
    )
    return pl.pallas_call(
        finish_kernel,
        grid=(2,),
        out_shape=(jax.ShapeDtypeStruct((LENGTH, D), BF16), f32(LENGTH, D))
        + tuple(f32(*shape) for shape in shapes),
        in_specs=[
            pl.BlockSpec((1, 512, D), lambda i: (0, i, 0)),
            pl.BlockSpec((1, 512, D), lambda i: (1, i, 0)),
            whole(3072, 128),
            whole(8, 128),
        ],
        out_specs=(spec, spec) + tuple(whole(*shape) for shape in shapes),
        compiler_params=pltpu.CompilerParams(vmem_limit_bytes=56 << 20),
        cost_estimate=pl.CostEstimate(flops=0, bytes_accessed=28 << 20, transcendentals=0),
    )(both, both, pieces, small)


def per_device(
    inputs, norm_gain, norm_bias, attn_weight, attn_bias, dense_weight, dense_bias,
    expand_weight, expand_bias, shrink_weight, shrink_bias, cotangent,
):
    both, pieces, small = run_layer(
        inputs, cotangent, shrink_weight, dense_weight, expand_weight, attn_weight,
        norm_gain, norm_bias, expand_bias, attn_bias, dense_bias, shrink_bias,
    )
    return finish(both, pieces, small)


def solution(mesh):
    placed = (
        P("dp", None),
        P(),
        P(),
        P(None, None, "tensor"),
        P(None, "tensor"),
        P("tensor", None),
        P(),
        P(None, "tensor"),
        P("tensor"),
        P("tensor", None),
        P(),
        P("dp", None),
    )
    return jax.shard_map(
        per_device,
        mesh=mesh,
        in_specs=placed,
        out_specs=(
            P("dp", None),
            P("dp", None),
            P("dp"),
            P("dp"),
            P(None, "dp", "tensor"),
            P(None, ("tensor", "dp")),
            P("tensor", "dp"),
            P("dp"),
            P("dp", "tensor"),
            P(("tensor", "dp")),
            P("tensor", "dp"),
            P("dp"),
        ),
        check_vma=False,
    )
```

time: 373 us -> 196 us (0.53); the launches traced: 369 us -> 196 us
  blocking collectives: 64.6 us -> 0 us
  matrix products: 46.4 us -> 0 us
  other arithmetic: 32.5 us -> 0 us
  local copies, waits for them, and re-layouts: 25.3 us -> 0 us
  Pallas kernels: 170 us -> 195 us
  between operations: 16 us -> 0.66 us
  waiting for transfers between devices: 14.6 us -> 0 us
    dot_general x16 -> x0, matrix products: 46.4 us -> none  [the longest x1 13 us: per_device(): jnp.einsum('td,fd->tf', cotangent, shrink_weight, preferred_element_type=...]
    unnamed x1 -> x0, blocking collectives: 38.8 us -> none
    psum x1 -> x0, blocking collectives: 25.8 us -> none  [per_device(): both = lax.psum(sums[:2], 'tensor')]
    pallas_call x1 -> x2, Pallas kernels: 170 us -> 195 us  [the longest x1 184 us: run_layer(): pl.pallas_call(layer_kernel, out_shape=(jax.ShapeDtypeStruct((2, LENGTH,...]
    convert_element_type x9 -> x0, other arithmetic: 18.4 us -> none  [the longest x2 8.89 us: per_device(): grad_scores = (chances * (grad_chances - row_dot)).astype(jnp.bfloat16)]
    unnamed x50 -> x0, local copies, waits for them, and re-layouts: 15.8 us -> none
    unnamed x2 -> x0, waiting for transfers between devices: 14.6 us -> none
    reduce_sum x6 -> x0, other arithmetic: 10.4 us -> none  [the longest x2 3.34 us: per_device(): row_total = jnp.sum(expo, axis=-1, keepdims=True)]
  transfers between devices with their start and end apart: 1 -> 0, of which waited for: 1 -> 0; matrix products, arithmetic and copies ran while one was open for 4% -> 0% of each run, Pallas kernels for 0% -> 0%
where the time goes in v1:
time: 196 us
  Pallas kernels  195 us (99%)
    pallas_call x1, Pallas kernels, run_layer(): pl.pallas_call(layer_kernel, out_shape=(jax.ShapeDtypeStruct((2, LENGTH,...  184 us
    pallas_call x1, Pallas kernels, finish(): pl.pallas_call(finish_kernel, grid=(2,), out_shape=(jax.ShapeDtypeStruct(...  11.6 us

profile of v1, /device:TPU:0, one launch (start us, length us, event | category | flops | bytes accessed | tf_op | source)
XLA Modules:
  0.0 196.1 jit_solution(11609682697536001287)
XLA Ops:
  0.6 183.8 %shard_map.229 = (f32[2,1024,2048]{2,1,0:T(8,128)}, f32[3072,128]{1,0:T(8,128)}, f32[8,128]{1,0:T(8,128)}) custom-call(bf16[1024,2048]{1,0:T(8,128)(2,1)} %x_hbm.1, bf16[1024,2048]{1,0:T(8,128)(2,1)} %g_hbm.1, bf16[1024,2048]{1,0:T(8,128)(2,1)} %sw_hbm.1, bf16[256,2048]{1,0:T(8,128)(2,1)} %dw_hbm.1, bf16[2048,1024]{1,0:T(8,128)(2,1)} %ew_hbm.1, ...), custom_call_target="tpu_custom_call" | custom-call | flops 21474836480 | bytes 62914560 | tf_op jit(solution)/shard_map/pallas_call | solution.py:770
  184.5 11.6 %shard_map.230 = (bf16[1024,2048]{1,0:T(8,128)(2,1)}, f32[1024,2048]{1,0:T(8,128)}, f32[128]{0:T(128)}, f32[128]{0:T(128)}, f32[3,128,256]{2,1,0:T(8,128)}, /*in...) custom-call(f32[2,1024,2048]{2,1,0:T(8,128)} %get-tuple-element.15.g, ...), custom_call_target="tpu_custom_call" | custom-call | bytes 29360128 | tf_op jit(solution)/shard_map/pallas_call | solution.py:902

commit v2 on v1

--- a/solution.py
+++ b/solution.py
@@ -27,7 +27,7 @@
 KZ = 5
 KT = 8
 KG = 4
-TICKS = 23
+TICKS = 24
 
 
 def gelu_parts(v):
@@ -635,8 +635,12 @@
     def at_least(k, bound):
         return jnp.where(k >= bound, 1, 0)
 
-    def between(h, first, last):
-        return (h >= first) & (h <= last)
+    def at_steps(h, steps, body):
+        first, count = 0, 0
+        for step in steps:
+            first += jnp.where(h > step, 1, 0)
+            count += jnp.where(h == step, 1, 0)
+        pl.loop(first, first + count)(body)
 
     def stage(t, late, body):
         when((t >= late) & (t < late + 16), body, t - late)
@@ -662,8 +666,8 @@
             def _():
                 stage(t, 6, z5)
                 stage(t, 1, z1)
-                stage(t, 7, x4)
-                stage(t, 2, x0)
+                stage(t, 8, x4)
+                stage(t, 3, x0)
                 when(t == 19, v1)
                 when(t == 20, v3)
 
@@ -671,12 +675,12 @@
             def _():
                 stage(t, 7, z6)
                 stage(t, 2, z2)
-                stage(t, 3, x1)
+                stage(t, 4, x1)
 
             @pl.when(pos == 2)
             def _():
                 stage(t, 3, z3)
-                stage(t, 4, x2)
+                stage(t, 5, x2)
                 when(t == 18, v0)
                 when(t == 19, v2)
                 when(t == 20, v4)
@@ -684,13 +688,13 @@
             @pl.when(pos == 3)
             def _():
                 stage(t, 4, z4)
-                stage(t, 5, x3)
-
-            @pl.when(t < UNITS)
+                stage(t, 6, x3)
+
+            @pl.when(t < UNITS + 1)
             def _():
-                when((pos > 0) & (pos < 3) & (t % 2 == 0), partial, t, pos - 1)
-                when(pos == 2, lambda: cross(t).start())
-                w = t - 1
+                when((pos > 0) & (pos < 3) & (t % 2 == 0) & (t < UNITS), partial, t, pos - 1)
+                when((pos == 2) & (t < UNITS), lambda: cross(t).start())
+                w = t - 2
                 when(
                     (pos >= 2) & (w >= 0) & (w % 4 < 3),
                     lambda: block(w // 4 * 3 + w % 4, pos - 2),
@@ -722,29 +726,11 @@
                     for k in (5, 6, 7):
                         load(k).wait()
 
-                first = jnp.where(h <= 3, 0, jnp.where(h <= 5, 1, 3))
-                pl.loop(
-                    first,
-                    first + jnp.where(h == 5, 2, jnp.where((h == 3) | (h == 7), 1, 0)),
-                )(lambda j: expand_part(pl.ds(CH, LENGTH - CH), j))
-                first = jnp.where(h <= 2, 0, jnp.where(h == 3, 2, jnp.where(h <= 4, 4, h - 2)))
-                pl.loop(
-                    first,
-                    first
-                    + jnp.where(
-                        (h == 0) | (h == 3), 2, jnp.where((h == 4) | between(h, 7, 15), 1, 0)
-                    ),
-                )(attend_item)
-                when(between(h, 18, 19) | between(h, 23, 24), hidden_back, jnp.where(h < 20, h - 18, h - 21))
-                back = jnp.where(
-                    h <= 30, h - 27, jnp.where(h <= 36, h - 30, jnp.where(h <= 43, h - 35, 9))
-                )
-                when(
-                    between(h, 27, 30) | between(h, 34, 36) | between(h, 42, 43) | (h == 53),
-                    back_item,
-                    back,
-                )
-                when(h == 54, token_sums)
+                at_steps(h, (3, 4, 6, 7), lambda j: expand_part(pl.ds(CH, LENGTH - CH), j))
+                at_steps(h, (0, 0, 5, 5, 8, 9, 11, 12, 13, 14, 15, 16, 17, 18), attend_item)
+                at_steps(h, (19, 20, 21, 24), hidden_back)
+                at_steps(h, (28, 29, 31, 32, 36, 37, 40, 44, 45, 52), back_item)
+                when(h == 53, token_sums)
                 when(h == 0, load(8).wait)
 
 
@@ -894,19 +880,19 @@
     def f32(*shape):
         return jax.ShapeDtypeStruct(shape, F32)
 
-    spec = pl.BlockSpec((512, D), lambda i: (i, 0))
+    spec = pl.BlockSpec((256, D), lambda i: (i, 0))
     shapes = (
         (128,), (128,), (3, 128, 256), (3, 16), (256, 128), (128,), (128, 1024), (64,), (1024, 128),
         (128,),
     )
     return pl.pallas_call(
         finish_kernel,
-        grid=(2,),
+        grid=(4,),
         out_shape=(jax.ShapeDtypeStruct((LENGTH, D), BF16), f32(LENGTH, D))
         + tuple(f32(*shape) for shape in shapes),
         in_specs=[
-            pl.BlockSpec((1, 512, D), lambda i: (0, i, 0)),
-            pl.BlockSpec((1, 512, D), lambda i: (1, i, 0)),
+            pl.BlockSpec((1, 256, D), lambda i: (0, i, 0)),
+            pl.BlockSpec((1, 256, D), lambda i: (1, i, 0)),
             whole(3072, 128),
             whole(8, 128),
         ],

time: 196 us -> 193 us (0.985)
  Pallas kernels: 195 us -> 192 us
    pallas_call x1, Pallas kernels: 184 us -> 181 us  [run_layer(): pl.pallas_call(layer_kernel, out_shape=(jax.ShapeDtypeStruct((2, LENGTH,...]
where the time goes in v2:
time: 193 us
  Pallas kernels  192 us (99%)
    pallas_call x1, Pallas kernels, run_layer(): pl.pallas_call(layer_kernel, out_shape=(jax.ShapeDtypeStruct((2, LENGTH,...  181 us
    pallas_call x1, Pallas kernels, finish(): pl.pallas_call(finish_kernel, grid=(4,), out_shape=(jax.ShapeDtypeStruct(...  11.2 us

profile of v2, /device:TPU:0, one launch (start us, length us, event | category | flops | bytes accessed | tf_op | source)
XLA Modules:
  0.0 192.5 jit_solution(9719465760220151166)
XLA Ops:
  0.6 180.6 %shard_map.229 = (f32[2,1024,2048]{2,1,0:T(8,128)}, f32[3072,128]{1,0:T(8,128)}, f32[8,128]{1,0:T(8,128)}) custom-call(bf16[1024,2048]{1,0:T(8,128)(2,1)} %x_hbm.1, bf16[1024,2048]{1,0:T(8,128)(2,1)} %g_hbm.1, bf16[1024,2048]{1,0:T(8,128)(2,1)} %sw_hbm.1, bf16[256,2048]{1,0:T(8,128)(2,1)} %dw_hbm.1, bf16[2048,1024]{1,0:T(8,128)(2,1)} %ew_hbm.1, ...), custom_call_target="tpu_custom_call" | custom-call | flops 21474836480 | bytes 62914560 | tf_op jit(solution)/shard_map/pallas_call | solution.py:756
  181.3 11.2 %shard_map.230 = (bf16[1024,2048]{1,0:T(8,128)(2,1)}, f32[1024,2048]{1,0:T(8,128)}, f32[128]{0:T(128)}, f32[128]{0:T(128)}, f32[3,128,256]{2,1,0:T(8,128)}, /*in...) custom-call(f32[2,1024,2048]{2,1,0:T(8,128)} %get-tuple-element.15.g, ...), custom_call_target="tpu_custom_call" | custom-call | bytes 29360128 | tf_op jit(solution)/shard_map/pallas_call | solution.py:888

commit v3 on v2

--- a/solution.py
+++ b/solution.py
@@ -312,6 +312,13 @@
 
     def z3(u):
         slot = u % KZ
+
+        def send():
+            for d in (0, 1):
+                gather1(d, u).start()
+            twin(0, u).start()
+            keep(0, u).start()
+
         for d in (0, 1):
             along(1, d, u).wait_recv()
             along(2, d, u).wait_recv()
@@ -325,6 +332,7 @@
         @pl.when(u < 8)
         def _():
             done[u % 2] = states + whole + vec_ref[2:3, :]
+            send()
 
         @pl.when(u >= 8)
         def _():
@@ -339,13 +347,10 @@
                 - jnp.mean(e, axis=-1, keepdims=True)
                 - zz * jnp.mean(e * zz, axis=-1, keepdims=True)
             )
+            send()
             gs_ref[0:1, :] += jnp.sum(whole * zz, axis=0, keepdims=True)
             gs_ref[1:2, :] += jnp.sum(whole, axis=0, keepdims=True)
 
-        for d in (0, 1):
-            gather1(d, u).start()
-        twin(0, u).start()
-        keep(0, u).start()
         for kind in (0, 1, 2):
             for d in (0, 1):
                 along(kind, d, u).wait_send()

time: 193 us -> 193 us (level)
  no operation moved by 1% of the time
where the time goes in v3:
time: 193 us
  Pallas kernels  192 us (99%)
    pallas_call x1, Pallas kernels, run_layer(): pl.pallas_call(layer_kernel, out_shape=(jax.ShapeDtypeStruct((2, LENGTH,...  181 us
    pallas_call x1, Pallas kernels, finish(): pl.pallas_call(finish_kernel, grid=(4,), out_shape=(jax.ShapeDtypeStruct(...  11.2 us

profile of v3, /device:TPU:0, one launch (start us, length us, event | category | flops | bytes accessed | tf_op | source)
XLA Modules:
  0.0 192.5 jit_solution(5070579986390134667)
XLA Ops:
  0.6 180.6 %shard_map.229 = (f32[2,1024,2048]{2,1,0:T(8,128)}, f32[3072,128]{1,0:T(8,128)}, f32[8,128]{1,0:T(8,128)}) custom-call(bf16[1024,2048]{1,0:T(8,128)(2,1)} %x_hbm.1, bf16[1024,2048]{1,0:T(8,128)(2,1)} %g_hbm.1, bf16[1024,2048]{1,0:T(8,128)(2,1)} %sw_hbm.1, bf16[256,2048]{1,0:T(8,128)(2,1)} %dw_hbm.1, bf16[2048,1024]{1,0:T(8,128)(2,1)} %ew_hbm.1, ...), custom_call_target="tpu_custom_call" | custom-call | flops 21474836480 | bytes 62914560 | tf_op jit(solution)/shard_map/pallas_call | solution.py:761
  181.3 11.2 %shard_map.230 = (bf16[1024,2048]{1,0:T(8,128)(2,1)}, f32[1024,2048]{1,0:T(8,128)}, f32[128]{0:T(128)}, f32[128]{0:T(128)}, f32[3,128,256]{2,1,0:T(8,128)}, /*in...) custom-call(f32[2,1024,2048]{2,1,0:T(8,128)} %get-tuple-element.15.g, ...), custom_call_target="tpu_custom_call" | custom-call | bytes 29360128 | tf_op jit(solution)/shard_map/pallas_call | solution.py:893
